TPU v7x, 32 devices: a whole 2x2x4 slice. The times are simulated.
32 devices in a mesh: groups: 2 (over y), tm: 4 (over z), tile: 2 (over x), arrow: 2 (over core).
Axes of the slice: x: 2, y: 2, z: 4, core: 2. Of those that a mesh axis runs over, the one named last changes fastest.
Arguments:
- forward_blocks: float32 [8, 96, 1024], P(('groups', 'tm'), ('tile', 'arrow')), parts along dimension 0, may hold values from -3 to 3
- arrow_rhs: float32 [192, 64], P(('groups', 'tile', 'arrow')), parts along dimension 0, may hold values from -6 to 6
- diag_inverse: bfloat16 [8, 1024, 1024], P(('groups', 'tm'), None, ('tile', 'arrow')), parts along dimension 0
- lower_coupling: bfloat16 [8, 1024, 1024], P(('groups', 'tm'), None, ('tile', 'arrow')), parts along dimension 0
- arrow_slab: bfloat16 [8, 64, 1024], P(('groups', 'tm'), 'arrow'), parts along dimension 0, may hold values from -0.09375 to 0.09375
- arrow_inverse: float32 [128, 64], P('groups'), parts along dimension 0
- boundary_term: float32 [192, 1024], P(('groups', 'tile', 'arrow')), parts along dimension 0, may hold values from -6 to 6
Outputs:
- solution: float32 [8, 96, 1024], P(('groups', 'tm'), ('tile', 'arrow')), parts along dimension 0
- arrow_solution: float32 [192, 64], P(('groups', 'tile', 'arrow')), parts along dimension 0
There are 2 independent parts, one for each index of `groups`. A program takes and returns all parts, laid end to end along the dimension named above; each array names one. Nothing has to cross between parts.
All inputs are finite; a program needn't handle non-finite values.
Results may differ from a plain program's by a relative error of at most 0.007.
Values may be sent and summed in bfloat16 or wider, within the bound.
A program may use at most 64 MiB of HBM per device.

v0:
```python
import jax
import jax.numpy as jnp
from jax import lax
from jax.sharding import PartitionSpec as P


def from_behind(block, axis, distance):
    devices = range(lax.axis_size(axis))
    route = [(i - distance, i) for i in devices if i - distance in devices]
    return lax.ppermute(block, axis, route)


def shards(
    forward_blocks,
    arrow_rhs,
    diag_inverse,
    lower_coupling,
    arrow_slab,
    arrow_inverse,
    boundary_term,
):
    highest = lax.Precision.HIGHEST
    slab_full = lax.all_gather(arrow_slab, "arrow", axis=1, tiled=True)
    slab_wide = slab_full[0].astype(jnp.float32)
    block_rows = forward_blocks[0]
    local_part = jnp.dot(block_rows, slab_wide.T, precision=highest)
    arrow_sum = lax.psum(local_part, "tm")
    arrow_forward = jnp.dot(arrow_rhs - arrow_sum, arrow_inverse.T, precision=highest)
    arrow_solution = jnp.dot(arrow_forward, arrow_inverse, precision=highest)
    arrow_term = jnp.dot(arrow_solution, slab_wide, precision=highest)
    source_rows = block_rows - arrow_term
    inverse_full, lower_full = (
        lax.all_gather(diag_inverse, ("tile", "arrow"), axis=2, tiled=True),
        lax.all_gather(lower_coupling, ("tile", "arrow"), axis=2, tiled=True),
    )
    coupling = jnp.dot(inverse_full[0], lower_full[0], preferred_element_type=jnp.float32).astype(
        jnp.bfloat16
    )
    coupling_wide = coupling.astype(jnp.float32)
    is_last = (lax.axis_index("tm") == lax.axis_size("tm") - 1).astype(jnp.float32)
    entry_term = is_last * boundary_term

    def one_turn(turn_index, carry_in):
        residual = source_rows - carry_in
        outgoing = jnp.dot(residual, coupling_wide, precision=highest)
        return entry_term + from_behind(outgoing, "tm", -1)

    carry_in = lax.fori_loop(0, lax.axis_size("tm") - 1, one_turn, entry_term)
    residual = source_rows - carry_in
    solution = jnp.dot(
        residual.astype(jnp.bfloat16), inverse_full[0], preferred_element_type=jnp.float32
    )
    return (solution[None], arrow_solution)


def solution(mesh):
    return jax.shard_map(
        shards,
        mesh=mesh,
        in_specs=(
            P(("groups", "tm"), ("tile", "arrow"), None),
            P(("groups", "tile", "arrow"), None),
            P(("groups", "tm"), None, ("tile", "arrow")),
            P(("groups", "tm"), None, ("tile", "arrow")),
            P(("groups", "tm"), "arrow", None),
            P("groups", None),
            P(("groups", "tile", "arrow"), None),
        ),
        out_specs=(
            P(("groups", "tm"), ("tile", "arrow"), None),
            P(("groups", "tile", "arrow"), None),
        ),
        check_vma=False,
    )
```

profile of v0, /device:TPU:0, one launch (start us, length us, event | category | flops | bytes accessed | tf_op | source)
XLA Modules:
  0.0 106.9 jit_solution(2100586051761688842)
XLA Ops:
  7.2 0.0 copy-start
  7.2 0.0 copy-start.2
  7.2 0.0 all-gather.3.cloned.1.call-start
  7.2 0.7 all-gather.3.cloned.1.call-update
  7.9 0.0 all-gather.5.cloned.1.call-start
  8.0 0.7 all-gather.5.cloned.1.call-update
  8.7 0.9 broadcast_multiply_fusion
  9.6 2.2 %all_gather.9 = bf16[1,64,1024]{2,1,0:T(8,128)(2,1)S(1)} all-gather(bf16[1,32,1024]{2,1,0:T(8,128)(2,1)} %param.13), channel_id=1, replica_groups=mesh['groups'=2,'tm'=4,'tile'=2,'arrow'=2] {'arrow'}, dimensions={1}, use_global_device_ids=true | all-gather | bytes 196608 | tf_op jit(solution)/shard_map/all_gather | solution.py:23
  11.8 1.1 fusion.15
  12.9 20.3 %psum.7 = f32[24,64]{1,0:T(8,128)S(1)} all-reduce(f32[24,64]{1,0:T(8,128)S(1)} %fusion.15), channel_id=1, replica_groups=mesh['groups'=2,'tm'=4,'tile'=2,'arrow'=2] {'tm'}, use_global_device_ids=true, to_apply=%region_0.0 | all-reduce | flops 1536 | bytes 12288 | tf_op jit(solution)/shard_map/psum | solution.py:27
  33.2 0.0 copy-done
  33.2 0.9 fusion.18
  34.1 0.2 fusion.20
  34.2 0.0 copy-done.2
  34.3 0.0 copy-start.3
  34.3 0.2 convolution_subtract_fusion
  34.5 0.7 all-gather.3.cloned.1.call-done
  35.1 24.4 %all-gather.5.cloned.1.call-done = bf16[1,1024,1024]{2,1,0:T(8,128)(2,1)} async-done(((bf16[1,1024,256]{2,1,0:T(8,128)(2,1)}), bf16[1,1024,1024]{2,1,0:T(8,128)(2,1)}) %all-gather.5.cloned.1.call-update) | async-done | bytes 2097168 | tf_op jit(solution)/shard_map/all_gather | solution.py:34
  59.6 6.5 %convert_convert_fusion = f32[1024,1024]{1,0:T(8,128)} fusion(bf16[1,1024,1024]{2,1,0:T(8,128)(2,1)} %all-gather.5.cloned.1.call-done, bf16[1,1024,1024]{2,1,0:T(8,128)(2,1)} %all-gather.3.cloned.1.call-done), kind=kOutput, calls=%fused_computation.7 | convolution fusion | flops 2149580800 | bytes 8388608 | tf_op jit(solution)/shard_map/dot_general | solution.py:36
  66.1 0.0 copy-done.3
  66.1 32.9 %while.10 = (s32[]{:T(128)}, f32[24,1024]{1,0:T(8,128)S(1)}, f32[24,1024]{1,0:T(8,128)S(1)}, f32[1024,1024]{1,0:T(8,128)}, f32[24,1024]{1,0:T(8,128)S(1)}, /*index=5*/s32[]{:T(128)}) while((s32[]{:T(128)}, f32[24,1024]{1,0:T(8,128)S(1)}, f32[24,1024]{1,0:T(8,128)S(1)}, f32[1024,1024]{1,0:T(8,128)}, f32[24,1024]{1,0:T(8,128)S(1)}, ...), condition=%wide.region_2.0_spmd, body=%wide.region_1.0_spmd.sunk | while | flops 302039040 | bytes 5177453 | solution.py:48
  66.1 4.4 %fusion.31 = f32[24,1024]{1,0:T(8,128)S(1)} fusion(f32[1024,1024]{1,0:T(8,128)} %get-tuple-element.86, f32[24,1024]{1,0:T(8,128)S(1)} %get-tuple-element.85, f32[24,1024]{1,0:T(8,128)S(1)} %get-tuple-element.78), kind=kOutput, calls=%fused_computation.clone.1 | convolution fusion | flops 302014464 | bytes 4489216 | tf_op jit(solution)/shard_map/while/body/eval_jaxpr/dot_general | solution.py:45
  70.5 1.3 %collective-permute-start = (f32[24,1024]{1,0:T(8,128)S(1)}, f32[24,1024]{1,0:T(8,128)S(1)}, u32[]{:S(2)}, u32[]{:S(2)}) collective-permute-start(f32[24,1024]{1,0:T(8,128)S(1)} %fusion.31), channel_id=1, source_target_pairs={{4,0},{8,4},{12,8},{5,1},{9,5},{13,9},{6,2},{10,6},{14,10},{7,3},{... | collective-permute-start | bytes 294920 | tf_op jit(solution)/shard_map/while/body/eval_jaxpr/ppermute | solution.py:10
  71.8 5.6 %collective-permute-done = f32[24,1024]{1,0:T(8,128)S(1)} collective-permute-done((f32[24,1024]{1,0:T(8,128)S(1)}, f32[24,1024]{1,0:T(8,128)S(1)}, u32[]{:S(2)}, u32[]{:S(2)}) %collective-permute-start) | collective-permute-done | bytes 98336 | tf_op jit(solution)/shard_map/while/body/eval_jaxpr/ppermute | solution.py:10
  77.4 4.3 %fusion.31 = f32[24,1024]{1,0:T(8,128)S(1)} fusion(f32[1024,1024]{1,0:T(8,128)} %get-tuple-element.86, f32[24,1024]{1,0:T(8,128)S(1)} %get-tuple-element.85, f32[24,1024]{1,0:T(8,128)S(1)} %get-tuple-element.78), kind=kOutput, calls=%fused_computation.clone.1 | convolution fusion | flops 302014464 | bytes 4489216 | tf_op jit(solution)/shard_map/while/body/eval_jaxpr/dot_general | solution.py:45
  81.7 1.3 %collective-permute-start = (f32[24,1024]{1,0:T(8,128)S(1)}, f32[24,1024]{1,0:T(8,128)S(1)}, u32[]{:S(2)}, u32[]{:S(2)}) collective-permute-start(f32[24,1024]{1,0:T(8,128)S(1)} %fusion.31), channel_id=1, source_target_pairs={{4,0},{8,4},{12,8},{5,1},{9,5},{13,9},{6,2},{10,6},{14,10},{7,3},{... | collective-permute-start | bytes 294920 | tf_op jit(solution)/shard_map/while/body/eval_jaxpr/ppermute | solution.py:10
  83.0 5.2 %collective-permute-done = f32[24,1024]{1,0:T(8,128)S(1)} collective-permute-done((f32[24,1024]{1,0:T(8,128)S(1)}, f32[24,1024]{1,0:T(8,128)S(1)}, u32[]{:S(2)}, u32[]{:S(2)}) %collective-permute-start) | collective-permute-done | bytes 98336 | tf_op jit(solution)/shard_map/while/body/eval_jaxpr/ppermute | solution.py:10
  88.2 4.3 %fusion.31 = f32[24,1024]{1,0:T(8,128)S(1)} fusion(f32[1024,1024]{1,0:T(8,128)} %get-tuple-element.86, f32[24,1024]{1,0:T(8,128)S(1)} %get-tuple-element.85, f32[24,1024]{1,0:T(8,128)S(1)} %get-tuple-element.78), kind=kOutput, calls=%fused_computation.clone.1 | convolution fusion | flops 302014464 | bytes 4489216 | tf_op jit(solution)/shard_map/while/body/eval_jaxpr/dot_general | solution.py:45
  92.5 1.3 %collective-permute-start = (f32[24,1024]{1,0:T(8,128)S(1)}, f32[24,1024]{1,0:T(8,128)S(1)}, u32[]{:S(2)}, u32[]{:S(2)}) collective-permute-start(f32[24,1024]{1,0:T(8,128)S(1)} %fusion.31), channel_id=1, source_target_pairs={{4,0},{8,4},{12,8},{5,1},{9,5},{13,9},{6,2},{10,6},{14,10},{7,3},{... | collective-permute-start | bytes 294920 | tf_op jit(solution)/shard_map/while/body/eval_jaxpr/ppermute | solution.py:10
  93.8 5.2 %collective-permute-done = f32[24,1024]{1,0:T(8,128)S(1)} collective-permute-done((f32[24,1024]{1,0:T(8,128)S(1)}, f32[24,1024]{1,0:T(8,128)S(1)}, u32[]{:S(2)}, u32[]{:S(2)}) %collective-permute-start) | collective-permute-done | bytes 98336 | tf_op jit(solution)/shard_map/while/body/eval_jaxpr/ppermute | solution.py:10
  99.0 0.0 copy-done.1
  99.0 1.0 fusion.11
  (5 shorter events, 0.0 us)
Async XLA Ops:
  7.2 26.0 %copy-start = (f32[64,64]{1,0:T(8,128)S(1)}, f32[64,64]{1,0:T(8,128)}, u32[]{:S(2)}) copy-start(f32[64,64]{1,0:T(8,128)} %param.14) | copy-start | bytes 49156
  7.2 27.1 %copy-start.2 = (f32[1,24,1024]{2,1,0:T(8,128)S(1)}, f32[1,24,1024]{2,1,0:T(8,128)}, u32[]{:S(2)}) copy-start(f32[1,24,1024]{2,1,0:T(8,128)} %param.9) | copy-start | bytes 294916
  7.2 28.0 %all-gather.3.cloned.1.call-start = ((), (), s32[]{:S(2)}) async-start(), calls=%async_computation | async-start | bytes 2621440 | tf_op jit(solution)/shard_map/all_gather | solution.py:33
  7.9 51.6 %all-gather.5.cloned.1.call-start = ((), (), s32[]{:S(2)}) async-start(), calls=%async_computation.1 | async-start | bytes 2621440 | tf_op jit(solution)/shard_map/all_gather | solution.py:34
  34.3 31.8 %copy-start.3 = (f32[24,64]{1,0:T(8,128)}, f32[24,64]{1,0:T(8,128)S(1)}, u32[]{:S(2)}) copy-start(f32[24,64]{1,0:T(8,128)S(1)} %fusion.20) | copy-start | bytes 18436
  66.1 33.0 %copy-start.1 = (bf16[1,1024,1024]{2,1,0:T(8,128)(2,1)S(1)}, bf16[1,1024,1024]{2,1,0:T(8,128)(2,1)}, u32[]{:S(2)}) copy-start(bf16[1,1024,1024]{2,1,0:T(8,128)(2,1)} %all-gather.3.cloned.1.call-done) | copy-start | bytes 6291460
  70.5 6.8 %collective-permute-start = (f32[24,1024]{1,0:T(8,128)S(1)}, f32[24,1024]{1,0:T(8,128)S(1)}, u32[]{:S(2)}, u32[]{:S(2)}) collective-permute-start(f32[24,1024]{1,0:T(8,128)S(1)} %fusion.31), channel_id=1, source_target_pairs={{4,0},{8,4},{12,8},{5,1},{9,5},{13,9},{6,2},{10,6},{14,10},{7,3},{... | collective-permute-start | bytes 294920 | tf_op jit(solution)/shard_map/while/body/eval_jaxpr/ppermute | solution.py:10
  81.7 6.5 %collective-permute-start = (f32[24,1024]{1,0:T(8,128)S(1)}, f32[24,1024]{1,0:T(8,128)S(1)}, u32[]{:S(2)}, u32[]{:S(2)}) collective-permute-start(f32[24,1024]{1,0:T(8,128)S(1)} %fusion.31), channel_id=1, source_target_pairs={{4,0},{8,4},{12,8},{5,1},{9,5},{13,9},{6,2},{10,6},{14,10},{7,3},{... | collective-permute-start | bytes 294920 | tf_op jit(solution)/shard_map/while/body/eval_jaxpr/ppermute | solution.py:10
  92.5 6.5 %collective-permute-start = (f32[24,1024]{1,0:T(8,128)S(1)}, f32[24,1024]{1,0:T(8,128)S(1)}, u32[]{:S(2)}, u32[]{:S(2)}) collective-permute-start(f32[24,1024]{1,0:T(8,128)S(1)} %fusion.31), channel_id=1, source_target_pairs={{4,0},{8,4},{12,8},{5,1},{9,5},{13,9},{6,2},{10,6},{14,10},{7,3},{... | collective-permute-start | bytes 294920 | tf_op jit(solution)/shard_map/while/body/eval_jaxpr/ppermute | solution.py:10
Sparse Core Ops, SparseCore 0:
  9.6 25.5 all-gather.2
  36.7 22.8 all-gather.4
where the time goes:
time: 107 us
  waiting for transfers between devices  42.5 us (40%)
  matrix products  22.8 us (21%)
  blocking collectives  22.6 us (21%)
  between operations  14.1 us (13%)
  starting transfers between devices  3.94 us (4%)
    all_gather x1, waiting for transfers between devices, shards(): lax.all_gather(lower_coupling, ('tile', 'arrow'), axis=2, tiled=True)  24.4 us
    psum x1, blocking collectives, shards(): arrow_sum = lax.psum(local_part, 'tm')  20.3 us
    ppermute x3, waiting for transfers between devices, from_behind(): return lax.ppermute(block, axis, route)  16 us
    dot_general x3, matrix products, one_turn(): outgoing = jnp.dot(residual, coupling_wide, precision=highest)  13 us
    dot_general x1, matrix products, shards(): jnp.dot(inverse_full[0], lower_full[0], preferred_element_type=jnp.float32)  6.5 us
    ppermute x3, starting transfers between devices, from_behind(): return lax.ppermute(block, axis, route)  3.86 us
    all_gather x1, blocking collectives, shards(): slab_full = lax.all_gather(arrow_slab, 'arrow', axis=1, tiled=True)  2.21 us
  transfers between devices with their start and end apart: 5, of which 5 were waited for; matrix products, arithmetic and copies ran while one was open for 3% of the time, Pallas kernels for 0%

commit v1 on v0

--- a/solution.py
+++ b/solution.py
@@ -2,6 +2,25 @@
 import jax.numpy as jnp
 from jax import lax
 from jax.sharding import PartitionSpec as P
+
+
+def _test_area(x_local):
+    n = lax.axis_size(("tile", "arrow"))
+    frames = [(idx, (idx + 1) % n) for idx in range(n)]
+    even, x_next = ([x_local], [x_local])
+    series = [(idx, (idx - 1) % n) for idx in range(n)]
+    for _ in range(n // 2):
+        r2 = lax.ppermute(even[-1], ("tile", "arrow"), frames)
+        even.append(r2)
+    ii = 0
+    while ii < (n - 1) // 2:
+        new = lax.ppermute(x_next[-1], ("tile", "arrow"), series)
+        x_next.append(new)
+        ii += 1
+    reached = jnp.concatenate([*even[::-1], *x_next[1:]], axis=2)
+    step_out = lax.axis_index(("tile", "arrow"))
+    found_now = jnp.roll(reached, shift=(step_out - n // 2) * x_local.shape[2], axis=2)
+    return found_now
 
 
 def from_behind(block, axis, distance):
@@ -31,7 +50,7 @@
     source_rows = block_rows - arrow_term
     inverse_full, lower_full = (
         lax.all_gather(diag_inverse, ("tile", "arrow"), axis=2, tiled=True),
-        lax.all_gather(lower_coupling, ("tile", "arrow"), axis=2, tiled=True),
+        _test_area(lower_coupling),
     )
     coupling = jnp.dot(inverse_full[0], lower_full[0], preferred_element_type=jnp.float32).astype(
         jnp.bfloat16

time: 107 us -> 97.4 us (0.910)
  waiting for transfers between devices: 42.5 us -> 22.7 us
  local copies, waits for them, and re-layouts: 0.04 us -> 7.06 us
  starting transfers between devices: 3.94 us -> 6.45 us
    all_gather x1 -> x0, waiting for transfers between devices: 24.4 us -> none  [shards(): lax.all_gather(lower_coupling, ('tile', 'arrow'), axis=2, tiled=True)]
    ppermute x0 -> x3, waiting for transfers between devices: none -> 6.41 us  [the longest x2 6.41 us: _test_area(): r2 = lax.ppermute(even[-1], ('tile', 'arrow'), frames)]
    unnamed x9 -> x16, local copies, waits for them, and re-layouts: 0.04 us -> 6.17 us
    ppermute x0 -> x3, starting transfers between devices: none -> 2.55 us  [the longest x1 1.99 us: _test_area(): new = lax.ppermute(x_next[-1], ('tile', 'arrow'), series)]
  transfers between devices with their start and end apart: 5 -> 7, of which waited for: 5 -> 4; matrix products, arithmetic and copies ran while one was open for 3% -> 11% of each run, Pallas kernels for 0% -> 0%
where the time goes in v1:
time: 97.4 us; the launch traced here: 96.9 us
  matrix products  23.7 us (24%)
  waiting for transfers between devices  22.7 us (23%)
  blocking collectives  21.8 us (22%)
  between operations  14.2 us (15%)
  local copies, waits for them, and re-layouts  7.06 us (7%)
  starting transfers between devices  6.45 us (7%)
    psum x1, blocking collectives, shards(): arrow_sum = lax.psum(local_part, 'tm')  19.5 us
    ppermute x3, waiting for transfers between devices, from_behind(): return lax.ppermute(block, axis, route)  15.6 us
    dot_general x3, matrix products, one_turn(): outgoing = jnp.dot(residual, coupling_wide, precision=highest)  13 us
    dot_general x1, matrix products, shards(): jnp.dot(inverse_full[0], lower_full[0], preferred_element_type=jnp.float32)  6.5 us
    ppermute x2, waiting for transfers between devices, _test_area(): r2 = lax.ppermute(even[-1], ('tile', 'arrow'), frames)  6.41 us
    unnamed x16, local copies, waits for them, and re-layouts  6.17 us
    ppermute x3, starting transfers between devices, from_behind(): return lax.ppermute(block, axis, route)  3.86 us
    all_gather x1, blocking collectives, shards(): slab_full = lax.all_gather(arrow_slab, 'arrow', axis=1, tiled=True)  2.36 us
  transfers between devices with their start and end apart: 7, of which 4 were waited for; matrix products, arithmetic and copies ran while one was open for 11% of the time, Pallas kernels for 0%

profile of v1, /device:TPU:0, one launch (start us, length us, event | category | flops | bytes accessed | tf_op | source)
XLA Modules:
  0.0 96.9 jit_solution(5160209827441134845)
XLA Ops:
  7.2 0.7 all-gather.2.cloned.1.call-update
  7.9 0.5 collective-permute-start.1
  8.4 2.0 %collective-permute-start.3 = (bf16[1,1024,256]{2,1,0:T(8,128)(2,1)}, bf16[1,1024,256]{2,1,0:T(8,128)(2,1)S(1)}, u32[]{:S(2)}, u32[]{:S(2)}) collective-permute-start(bf16[1,1024,256]{2,1,0:T(8,128)(2,1)} %param.12), channel_id=1, source_target_pairs={{0,3},{1,0},{2,1},{3,2},{4,7},{5,4},{6,5},{7,6},{8,11},{9,8},{10,9... | collective-permute-start | bytes 1572872 | tf_op jit(solution)/shard_map/ppermute | solution.py:17
  10.4 2.4 %all_gather.6 = bf16[1,64,1024]{2,1,0:T(8,128)(2,1)S(1)} all-gather(bf16[1,32,1024]{2,1,0:T(8,128)(2,1)} %param.13), channel_id=1, replica_groups=mesh['groups'=2,'tm'=4,'tile'=2,'arrow'=2] {'arrow'}, dimensions={1}, use_global_device_ids=true | all-gather | bytes 196608 | tf_op jit(solution)/shard_map/all_gather | solution.py:42
  12.8 1.1 %fusion.16 = f32[24,64]{1,0:T(8,128)S(1)} fusion(bf16[1,64,1024]{2,1,0:T(8,128)(2,1)S(1)} %all_gather.6, f32[1,24,1024]{2,1,0:T(8,128)} %param.9), kind=kOutput, calls=%fused_computation.12 | convolution fusion | flops 18874368 | bytes 235520 | tf_op jit(solution)/shard_map/dot_general | solution.py:45
  13.8 19.5 %psum.7 = f32[24,64]{1,0:T(8,128)S(1)} all-reduce(f32[24,64]{1,0:T(8,128)S(1)} %fusion.16), channel_id=1, replica_groups=mesh['groups'=2,'tm'=4,'tile'=2,'arrow'=2] {'tm'}, use_global_device_ids=true, to_apply=%region_0.0 | all-reduce | flops 1536 | bytes 12288 | tf_op jit(solution)/shard_map/psum | solution.py:46
  33.3 0.9 broadcast_multiply_fusion
  34.2 0.1 collective-permute-start.2
  34.3 0.9 fusion.19
  35.2 0.1 fusion.22
  35.4 1.1 %convolution_subtract_fusion = f32[24,1024]{1,0:T(8,128)S(1)} fusion(f32[24,64]{1,0:T(8,128)S(1)} %fusion.22, bf16[1,64,1024]{2,1,0:T(8,128)(2,1)S(1)} %all_gather.6, f32[1,24,1024]{2,1,0:T(8,128)} %param.9), kind=kOutput, calls=%fused_computation.10 | convolution fusion | flops 18898944 | bytes 333824 | tf_op jit(solution)/shard_map/dot_general | solution.py:49
  36.5 6.4 %collective-permute-done.2 = bf16[1,1024,256]{2,1,0:T(8,128)(2,1)S(1)} collective-permute-done((bf16[1,1024,256]{2,1,0:T(8,128)(2,1)S(1)}, bf16[1,1024,256]{2,1,0:T(8,128)(2,1)S(1)}, u32[]{:S(2)}, u32[]{:S(2)}) %collective-permute-start.2) | collective-permute-done | bytes 524320 | tf_op jit(solution)/shard_map/ppermute | solution.py:13
  42.9 0.9 constant_dynamic-update-slice_fusion.7
  43.8 0.9 constant_dynamic-update-slice_fusion.6
  44.7 0.9 constant_dynamic-update-slice_fusion.5
  45.5 0.9 constant_dynamic-update-slice_fusion.4
  46.4 0.9 constant_dynamic-update-slice_fusion.3
  47.3 0.9 constant_dynamic-update-slice_fusion.2
  48.2 0.9 constant_dynamic-update-slice_fusion.1
  49.0 0.9 constant_dynamic-update-slice_fusion
  49.9 6.5 %convert_bitcast_fusion = f32[1024,1024]{1,0:T(8,128)} fusion(bf16[1,1024,2048]{2,1,0:T(8,128)(2,1)} %constant_dynamic-update-slice_fusion, s32[]{:T(128)S(6)} %select_n.14, bf16[1,1024,1024]{2,1,0:T(8,128)(2,1)} %all-gather.2.cloned.1.call-done), kind=kOutput, calls=%fused_computation.2 | convolution fusion | flops 2149580800 | bytes 8388612 | tf_op jit(solution)/shard_map/dot_general | solution.py:55
  56.4 32.6 %while.10 = (s32[]{:T(128)}, f32[24,1024]{1,0:T(8,128)S(1)}, f32[24,1024]{1,0:T(8,128)S(1)}, f32[1024,1024]{1,0:T(8,128)}, f32[24,1024]{1,0:T(8,128)S(1)}, /*index=5*/s32[]{:T(128)}) while((s32[]{:T(128)}, f32[24,1024]{1,0:T(8,128)S(1)}, f32[24,1024]{1,0:T(8,128)S(1)}, f32[1024,1024]{1,0:T(8,128)}, f32[24,1024]{1,0:T(8,128)S(1)}, ...), condition=%wide.region_2.3_spmd, body=%wide.region_1.2_spmd.sunk | while | flops 302039040 | bytes 5177453 | solution.py:67
  56.4 4.4 %fusion.33 = f32[24,1024]{1,0:T(8,128)S(1)} fusion(f32[1024,1024]{1,0:T(8,128)} %get-tuple-element.86, f32[24,1024]{1,0:T(8,128)S(1)} %get-tuple-element.85, f32[24,1024]{1,0:T(8,128)S(1)} %get-tuple-element.78), kind=kOutput, calls=%fused_computation.clone.1 | convolution fusion | flops 302014464 | bytes 4489216 | tf_op jit(solution)/shard_map/while/body/eval_jaxpr/dot_general | solution.py:64
  60.9 1.3 %collective-permute-start = (f32[24,1024]{1,0:T(8,128)S(1)}, f32[24,1024]{1,0:T(8,128)S(1)}, u32[]{:S(2)}, u32[]{:S(2)}) collective-permute-start(f32[24,1024]{1,0:T(8,128)S(1)} %fusion.33), channel_id=1, source_target_pairs={{4,0},{8,4},{12,8},{5,1},{9,5},{13,9},{6,2},{10,6},{14,10},{7,3},{... | collective-permute-start | bytes 294920 | tf_op jit(solution)/shard_map/while/body/eval_jaxpr/ppermute | solution.py:29
  62.2 5.2 %collective-permute-done = f32[24,1024]{1,0:T(8,128)S(1)} collective-permute-done((f32[24,1024]{1,0:T(8,128)S(1)}, f32[24,1024]{1,0:T(8,128)S(1)}, u32[]{:S(2)}, u32[]{:S(2)}) %collective-permute-start) | collective-permute-done | bytes 98336 | tf_op jit(solution)/shard_map/while/body/eval_jaxpr/ppermute | solution.py:29
  67.4 4.3 %fusion.33 = f32[24,1024]{1,0:T(8,128)S(1)} fusion(f32[1024,1024]{1,0:T(8,128)} %get-tuple-element.86, f32[24,1024]{1,0:T(8,128)S(1)} %get-tuple-element.85, f32[24,1024]{1,0:T(8,128)S(1)} %get-tuple-element.78), kind=kOutput, calls=%fused_computation.clone.1 | convolution fusion | flops 302014464 | bytes 4489216 | tf_op jit(solution)/shard_map/while/body/eval_jaxpr/dot_general | solution.py:64
  71.7 1.3 %collective-permute-start = (f32[24,1024]{1,0:T(8,128)S(1)}, f32[24,1024]{1,0:T(8,128)S(1)}, u32[]{:S(2)}, u32[]{:S(2)}) collective-permute-start(f32[24,1024]{1,0:T(8,128)S(1)} %fusion.33), channel_id=1, source_target_pairs={{4,0},{8,4},{12,8},{5,1},{9,5},{13,9},{6,2},{10,6},{14,10},{7,3},{... | collective-permute-start | bytes 294920 | tf_op jit(solution)/shard_map/while/body/eval_jaxpr/ppermute | solution.py:29
  73.0 5.2 %collective-permute-done = f32[24,1024]{1,0:T(8,128)S(1)} collective-permute-done((f32[24,1024]{1,0:T(8,128)S(1)}, f32[24,1024]{1,0:T(8,128)S(1)}, u32[]{:S(2)}, u32[]{:S(2)}) %collective-permute-start) | collective-permute-done | bytes 98336 | tf_op jit(solution)/shard_map/while/body/eval_jaxpr/ppermute | solution.py:29
  78.2 4.3 %fusion.33 = f32[24,1024]{1,0:T(8,128)S(1)} fusion(f32[1024,1024]{1,0:T(8,128)} %get-tuple-element.86, f32[24,1024]{1,0:T(8,128)S(1)} %get-tuple-element.85, f32[24,1024]{1,0:T(8,128)S(1)} %get-tuple-element.78), kind=kOutput, calls=%fused_computation.clone.1 | convolution fusion | flops 302014464 | bytes 4489216 | tf_op jit(solution)/shard_map/while/body/eval_jaxpr/dot_general | solution.py:64
  82.5 1.3 %collective-permute-start = (f32[24,1024]{1,0:T(8,128)S(1)}, f32[24,1024]{1,0:T(8,128)S(1)}, u32[]{:S(2)}, u32[]{:S(2)}) collective-permute-start(f32[24,1024]{1,0:T(8,128)S(1)} %fusion.33), channel_id=1, source_target_pairs={{4,0},{8,4},{12,8},{5,1},{9,5},{13,9},{6,2},{10,6},{14,10},{7,3},{... | collective-permute-start | bytes 294920 | tf_op jit(solution)/shard_map/while/body/eval_jaxpr/ppermute | solution.py:29
  83.8 5.2 %collective-permute-done = f32[24,1024]{1,0:T(8,128)S(1)} collective-permute-done((f32[24,1024]{1,0:T(8,128)S(1)}, f32[24,1024]{1,0:T(8,128)S(1)}, u32[]{:S(2)}, u32[]{:S(2)}) %collective-permute-start) | collective-permute-done | bytes 98336 | tf_op jit(solution)/shard_map/while/body/eval_jaxpr/ppermute | solution.py:29
  89.1 1.0 %fusion.12 = f32[1,24,1024]{2,1,0:T(8,128)} fusion(bf16[1,1024,1024]{2,1,0:T(8,128)(2,1)S(1)} %copy-done.1, f32[24,1024]{1,0:T(8,128)S(1)} %get-tuple-element.90, f32[24,1024]{1,0:T(8,128)S(1)} %get-tuple-element.29), kind=kOutput, calls=%fused_computation.9 | convolution fusion | flops 50380800 | bytes 2392064 | tf_op jit(solution)/shard_map/dot_general | solution.py:69
  (16 shorter events, 0.1 us)
Async XLA Ops:
  7.2 27.1 %copy-start = (f32[64,64]{1,0:T(8,128)S(1)}, f32[64,64]{1,0:T(8,128)}, u32[]{:S(2)}) copy-start(f32[64,64]{1,0:T(8,128)} %param.14) | copy-start | bytes 49156
  7.2 37.5 %copy-start.2 = (bf16[1,1024,256]{2,1,0:T(8,128)(2,1)S(1)}, bf16[1,1024,256]{2,1,0:T(8,128)(2,1)}, u32[]{:S(2)}) copy-start(bf16[1,1024,256]{2,1,0:T(8,128)(2,1)} %param.12) | copy-start | bytes 1572868
  7.2 42.7 %all-gather.2.cloned.1.call-start = ((), (), s32[]{:S(2)}) async-start(), calls=%async_computation | async-start | bytes 2621440 | tf_op jit(solution)/shard_map/all_gather | solution.py:52
  7.9 26.3 %collective-permute-start.1 = (bf16[1,1024,256]{2,1,0:T(8,128)(2,1)}, bf16[1,1024,256]{2,1,0:T(8,128)(2,1)S(1)}, u32[]{:S(2)}, u32[]{:S(2)}) collective-permute-start(bf16[1,1024,256]{2,1,0:T(8,128)(2,1)} %param.12), channel_id=1, source_target_pairs={{0,1},{1,2},{2,3},{3,0},{4,5},{5,6},{6,7},{7,4},{8,9},{9,10},{10,1... | collective-permute-start | bytes 1572872 | tf_op jit(solution)/shard_map/ppermute | solution.py:13
  8.4 37.1 %collective-permute-start.3 = (bf16[1,1024,256]{2,1,0:T(8,128)(2,1)}, bf16[1,1024,256]{2,1,0:T(8,128)(2,1)S(1)}, u32[]{:S(2)}, u32[]{:S(2)}) collective-permute-start(bf16[1,1024,256]{2,1,0:T(8,128)(2,1)} %param.12), channel_id=1, source_target_pairs={{0,3},{1,0},{2,1},{3,2},{4,7},{5,4},{6,5},{7,6},{8,11},{9,8},{10,9... | collective-permute-start | bytes 1572872 | tf_op jit(solution)/shard_map/ppermute | solution.py:17
  34.2 8.7 %collective-permute-start.2 = (bf16[1,1024,256]{2,1,0:T(8,128)(2,1)S(1)}, bf16[1,1024,256]{2,1,0:T(8,128)(2,1)S(1)}, u32[]{:S(2)}, u32[]{:S(2)}) collective-permute-start(bf16[1,1024,256]{2,1,0:T(8,128)(2,1)S(1)} %collective-permute-done.1), channel_id=1, source_target_pairs={{0,1},{1,2},{2,3},{3,0},{4,5},{5,6},{6,7},{7,4},{8,9},{9,10},{10,1... | collective-permute-start | bytes 1572872 | tf_op jit(solution)/shard_map/ppermute | solution.py:13
  35.4 14.5 %copy-start.3 = (f32[24,64]{1,0:T(8,128)}, f32[24,64]{1,0:T(8,128)S(1)}, u32[]{:S(2)}) copy-start(f32[24,64]{1,0:T(8,128)S(1)} %fusion.22) | copy-start | bytes 18436
  56.4 32.6 %copy-start.1 = (bf16[1,1024,1024]{2,1,0:T(8,128)(2,1)S(1)}, bf16[1,1024,1024]{2,1,0:T(8,128)(2,1)}, u32[]{:S(2)}) copy-start(bf16[1,1024,1024]{2,1,0:T(8,128)(2,1)} %all-gather.2.cloned.1.call-done) | copy-start | bytes 6291460
  60.9 6.5 %collective-permute-start = (f32[24,1024]{1,0:T(8,128)S(1)}, f32[24,1024]{1,0:T(8,128)S(1)}, u32[]{:S(2)}, u32[]{:S(2)}) collective-permute-start(f32[24,1024]{1,0:T(8,128)S(1)} %fusion.33), channel_id=1, source_target_pairs={{4,0},{8,4},{12,8},{5,1},{9,5},{13,9},{6,2},{10,6},{14,10},{7,3},{... | collective-permute-start | bytes 294920 | tf_op jit(solution)/shard_map/while/body/eval_jaxpr/ppermute | solution.py:29
  71.7 6.5 %collective-permute-start = (f32[24,1024]{1,0:T(8,128)S(1)}, f32[24,1024]{1,0:T(8,128)S(1)}, u32[]{:S(2)}, u32[]{:S(2)}) collective-permute-start(f32[24,1024]{1,0:T(8,128)S(1)} %fusion.33), channel_id=1, source_target_pairs={{4,0},{8,4},{12,8},{5,1},{9,5},{13,9},{6,2},{10,6},{14,10},{7,3},{... | collective-permute-start | bytes 294920 | tf_op jit(solution)/shard_map/while/body/eval_jaxpr/ppermute | solution.py:29
  82.5 6.5 %collective-permute-start = (f32[24,1024]{1,0:T(8,128)S(1)}, f32[24,1024]{1,0:T(8,128)S(1)}, u32[]{:S(2)}, u32[]{:S(2)}) collective-permute-start(f32[24,1024]{1,0:T(8,128)S(1)} %fusion.33), channel_id=1, source_target_pairs={{4,0},{8,4},{12,8},{5,1},{9,5},{13,9},{6,2},{10,6},{14,10},{7,3},{... | collective-permute-start | bytes 294920 | tf_op jit(solution)/shard_map/while/body/eval_jaxpr/ppermute | solution.py:29
Sparse Core Ops, SparseCore 0:
  9.6 26.8 all-gather.1
